TPU v7x, 32 devices: a whole 2x2x4 slice. The times are simulated.
32 devices in a mesh: gx: 8 (over z, y), gy: 4 (over x, core).
Axes of the slice: x: 2, y: 2, z: 4, core: 2. Of those that a mesh axis runs over, the one named last changes fastest.
Arguments:
- load_vectors: float32 [8, 4, 8, 8, 192], P('gx', 'gy'), may hold values from -45 to 45
- bond_stiffness: bfloat16 [8, 4, 8, 13, 36864], P('gx', 'gy'), may hold values from 0 to 0.0016937256
- intact_words: int32 [8, 4, 8, 13, 64, 4], P('gx', 'gy'), may hold values from 0 to 65535
- block_cols: int32 [8, 4, 8, 13], P('gx', 'gy'), may hold values from 0 to 89, as said below
- self_stiffness: bfloat16 [8, 4, 8, 36864], P('gx', 'gy'), may hold values from -0.01 to 3.01, as said below
- block_inverse: float32 [8, 4, 8, 36864], P('gx', 'gy'), may hold values from -0.01 to 0.61, as said below
- coarse_basis: float32 [8, 4, 16, 8, 192], P('gx', 'gy'), may hold values from -0.3 to 0.3
- coarse_factor: float32 [512, 512], P(('gx', 'gy')), may hold values from -0.5 to 0.5
Outputs:
- displacement: float32 [8, 4, 8, 8, 192], P('gx', 'gy')
- residual: float32 [8, 4, 8, 8, 192], P('gx', 'gy')
Inputs may be any that keep to these rules, and one draw needn't show every extreme that they name: `block_cols`: the 13 codes of a block name different blocks among the 26 around it (never the block itself), each |a - 1|, |c - 1|, |w - 1 - z| at most 1. `self_stiffness`: each block, read as a matrix, is symmetric. `block_inverse`: each block, read as a matrix, is symmetric.
All inputs are finite; a program needn't handle non-finite values.
Results may differ from a plain program's by a relative error of at most 0.0055.
Values may be sent and summed in bfloat16 or wider, within the bound.
A program may use at most 128 MiB of HBM per device.

v0:
```python
import jax
import jax.numpy as jnp
from jax import lax
from jax.sharding import PartitionSpec as P

COMP = 3
PB = 64
DOF = 192
NS = 13
BZ = 8
NLOAD = 8
ITERS = 2


highest = lax.Precision.HIGHEST


def padded_2(x, sides, width):
    for axis, dim in sides:
        size, length = (lax.axis_size(axis), x.shape[dim])
        up = [(i, (i + 1) % size) for i in range(size - 1)]
        down = [(j, i) for i, j in up]
        last = lax.slice_in_dim(x, length - width, length, axis=dim)
        initial = lax.slice_in_dim(x, 0, width, axis=dim)
        before = lax.ppermute(last, axis, up)
        after = lax.ppermute(initial, axis, down)
        x = jnp.concatenate([before, x, after], axis=dim)
    return x


def unpack_bits(packed):
    shifts = jnp.arange(16, dtype=jnp.int32)
    bitset = jnp.right_shift(packed[..., None], shifts) & 1
    return bitset.reshape(packed.shape[:-1] + (packed.shape[-1] * 16,))


def masked_blocks(stiffness, packed):
    intact = unpack_bits(packed).astype(stiffness.dtype)
    leading = stiffness.shape[:-1]
    shaped = stiffness.reshape(leading + (COMP, PB, COMP, PB))
    masked = shaped * intact[..., None, :, None, :]
    return masked.reshape(leading + (DOF, DOF))


def per_device(
    load_vectors,
    bond_stiffness,
    intact_words,
    block_cols,
    self_stiffness,
    block_inverse,
    coarse_basis,
    coarse_factor,
):
    weights = masked_blocks(bond_stiffness[0, 0], intact_words[0, 0])
    row_total = jnp.sum(weights, axis=(1, 3), dtype=jnp.float32)
    column_total = jnp.sum(weights, axis=2, dtype=jnp.float32)
    col_codes = block_cols[0, 0]
    depth_span = BZ + 2
    ghost_count = 9 * depth_span
    selector = (
        jnp.arange(ghost_count, dtype=jnp.int32)[:, None] == col_codes.reshape(-1)[None, :]
    ).astype(jnp.bfloat16)
    self_block = self_stiffness[0, 0].reshape(BZ, DOF, DOF)
    inverse = block_inverse[0, 0].reshape(BZ, DOF, DOF)
    coarse_vecs = coarse_basis[0, 0]

    def smooth_local(field):
        return jnp.einsum("bij,blj->bli", inverse, field, precision=highest)

    def restrict(field):
        restricted = jnp.einsum("kbi,bli->lk", coarse_vecs, field, precision=highest)
        return jnp.dot(restricted, coarse_factor, precision=highest)

    def prolong(summed):
        spread = jnp.einsum("lc,kc->lk", summed, coarse_factor, precision=highest)
        return jnp.einsum("kbi,lk->bli", coarse_vecs, spread, precision=highest)

    def precondition(residual):
        own_part = smooth_local(residual)
        coarse_term = restrict(residual)
        summed = lax.psum(coarse_term, ("gx", "gy"))
        smoothed = own_part + prolong(summed)
        energy = lax.psum(jnp.sum(residual * smoothed, axis=(0, 2)), ("gx", "gy"))
        return (smoothed, energy)

    residual = load_vectors[0, 0]
    solution = jnp.zeros_like(residual)
    smoothed, energy = precondition(residual)
    direction = smoothed
    for iteration in range(ITERS):
        rounded = direction.astype(jnp.bfloat16)
        ghosts = padded_2(rounded[None, None], (("gx", 0), ("gy", 1)), 1)
        padded = jnp.pad(ghosts, ((0, 0), (0, 0), (1, 1), (0, 0), (0, 0))).reshape(
            ghost_count, NLOAD, DOF
        )
        gathered = jnp.take(padded, col_codes, axis=0)
        forward = row_total[:, None, :] * rounded - jnp.einsum(
            "bsij,bslj->bli", weights, gathered, preferred_element_type=jnp.float32
        )
        backward = column_total[:, :, None, :] * gathered - jnp.einsum(
            "bsij,bli->bslj", weights, rounded, preferred_element_type=jnp.float32
        )
        flat_terms = backward.reshape(BZ * NS, NLOAD * DOF)
        high_part = flat_terms.astype(jnp.bfloat16)
        low_part = (flat_terms - high_part.astype(jnp.float32)).astype(jnp.bfloat16)
        apply_spread = jnp.dot(selector, high_part, preferred_element_type=jnp.float32) + jnp.dot(
            selector, low_part, preferred_element_type=jnp.float32
        )
        partial_value = apply_spread.reshape(3, 3, depth_span, NLOAD, DOF)[:, :, 1 : depth_span - 1]
        beside_all = padded_2(partial_value.astype(jnp.bfloat16), (("gx", 0), ("gy", 1)), 1).astype(
            partial_value.dtype
        )
        folded = (
            beside_all[2, 2]
            + beside_all[0, 0]
            + beside_all[0, 2]
            + beside_all[0, 4]
            + beside_all[2, 0]
        )
        folded = folded + beside_all[2, 4] + beside_all[4, 0] + beside_all[4, 2] + beside_all[4, 4]
        diagonal = jnp.einsum(
            "bij,blj->bli", self_block, rounded, preferred_element_type=jnp.float32
        )
        operator_out = diagonal + forward + folded
        curve_sum = lax.psum(jnp.sum(direction * operator_out, axis=(0, 2)), ("gx", "gy"))
        step_scale = (energy / curve_sum)[None, :, None]
        solution = solution + step_scale * direction
        residual = residual - step_scale * operator_out
        if iteration + 1 < ITERS:
            smoothed, new_energy = precondition(residual)
            direction = smoothed + (new_energy / energy)[None, :, None] * direction
            energy = new_energy
    return (solution[None, None], residual[None, None])


def solution(mesh):
    in_specs = (
        P("gx", "gy", None, None, None),
        P("gx", "gy", None, None, None),
        P("gx", "gy", None, None, None, None),
        P("gx", "gy", None, None),
        P("gx", "gy", None, None),
        P("gx", "gy", None, None),
        P("gx", "gy", None, None, None),
        P(("gx", "gy"), None),
    )
    out_specs = (P("gx", "gy", None, None, None), P("gx", "gy", None, None, None))
    return jax.shard_map(
        per_device, mesh=mesh, in_specs=in_specs, out_specs=out_specs, check_vma=False
    )
```

profile of v0, /device:TPU:0, one launch (start us, length us, event | category | flops | bytes accessed | tf_op | source)
XLA Modules:
  0.0 424.7 jit_solution(15320858401291001162)
XLA Ops:
  1.5 1.1 convolution_bitcast_fusion.5
  2.6 1.0 fusion.80
  3.5 42.0 %psum.42 = f32[8,512]{1,0:T(8,128)S(1)} all-reduce(f32[8,512]{1,0:T(8,128)S(1)} %fusion.80), channel_id=1, replica_groups=mesh['gx'=8,'gy'=4] {'gx','gy'}, use_global_device_ids=true, to_apply=%region_0.0 | all-reduce | flops 4096 | bytes 32768 | tf_op jit(solution)/shard_map/psum | solution.py:82
  46.5 2.0 reshape_squeeze.9
  48.5 2.2 fusion.63
  51.0 4.2 collective-permute-start
  55.2 1.3 collective-permute-start.1
  57.3 1.5 fusion.9
  58.8 2.9 copy.45
  61.7 8.8 %mul.97 = bf16[8,13,3,64,3,64]{5,4,3,2,1,0:T(4,128)(2,1)} broadcast(bf16[8,13,64,64]{3,2,1,0:T(8,128)(2,1)} %copy.45), dimensions={0,1,3,5} | broadcast | bytes 8519680 | tf_op jit(solution)/shard_map/mul | solution.py:41
  70.5 34.7 %mul.102 = bf16[8,13,192,192]{3,2,1,0:T(8,128)(2,1)} reshape(bf16[8,13,3,64,3,64]{5,4,3,2,1,0:T(4,128)(2,1)} %mul.97) | data formatting | bytes 15335424 | tf_op jit(solution)/shard_map/mul | solution.py:41
  105.1 16.7 %reshape_squeeze.11 = bf16[8,13,192,192]{3,2,0,1:T(8,128)(2,1)} reshape(bf16[1,1,8,13,36864]{4,2,3,1,0:T(8,128)(2,1)} %param.11) | data formatting | bytes 15335424 | tf_op jit(solution)/shard_map/reshape;squeeze | solution.py:40
  121.8 14.1 %convert_reduce_fusion = (f32[8,13,192]{2,0,1:T(8,128)S(1)}, bf16[8,13,192,192]{3,2,0,1:T(8,128)(2,1)}) fusion(bf16[8,13,192,192]{3,2,0,1:T(8,128)(2,1)} %reshape_squeeze.11, bf16[8,13,192,192]{3,2,1,0:T(8,128)(2,1)} %mul.102), kind=kLoop, calls=%fused_computation.2 | loop fusion | flops 11481600 | bytes 23083008 | tf_op jit(solution)/shard_map/reduce_sum | solution.py:57
  135.9 19.7 %reshape.113 = bf16[1,1,8,13,36864]{4,3,2,1,0:T(8,128)(2,1)} reshape(bf16[8,13,3,64,3,64]{5,4,3,2,1,0:T(4,128)(2,1)} %mul.97) | data formatting | bytes 15335424 | tf_op jit(solution)/shard_map/mul | solution.py:41
  156.6 1.3 collective-permute-start.2
  157.9 1.3 collective-permute-start.3
  159.2 2.6 collective-permute-done.3
  162.6 1.4 gather_fusion
  164.1 5.3 %fusion.21 = f32[8,13,8,192]{3,2,1,0:T(8,128)S(1)} fusion(bf16[8,13,192,192]{3,2,0,1:T(8,128)(2,1)} %get-tuple-element.11, f32[8,13,192]{2,1,0:T(8,128)S(1)} %copy.49, bf16[8,13,8,192]{3,2,1,0:T(8,128)(2,1)} %bitcast.123, pred[8,13]{1,0:T(8,128)(4,1)S(1)} %compare_and_fusion, bf16[8,8,192]{2,1,0:T(8,128)(2,1)S(1)} %get-tuple-element.22), kind=kOutput, calls=%fused_computation.24 | convolution fusion | flops 61980672 | bytes 8730728 | tf_op jit(solution)/shard_map/bsij,bli->bslj/dot_general | solution.py:101
  171.2 5.6 %collective-permute-start.4 = (bf16[1,3,8,8,192]{4,3,2,1,0:T(8,128)(2,1)}, bf16[1,3,8,8,192]{4,3,2,1,0:T(8,128)(2,1)}, u32[]{:S(2)}, u32[]{:S(2)}) collective-permute-start(bf16[1,3,8,8,192]{4,3,2,1,0:T(8,128)(2,1)} %get-tuple-element.18), channel_id=1, source_target_pairs={{0,4},{4,8},{8,12},{12,16},{16,20},{20,24},{24,28},{1,5},{5,9},{9,... | collective-permute-start | bytes 221192 | tf_op jit(solution)/shard_map/ppermute | solution.py:25
  176.8 1.5 collective-permute-start.5
  178.3 11.9 %convert_reduce_fusion.1 = f32[8,36864]{1,0:T(8,128)} fusion(bf16[1,1,8,13,36864]{4,2,3,1,0:T(8,128)(2,1)} %param.11, bf16[1,1,8,13,36864]{4,3,2,1,0:T(8,128)(2,1)} %reshape.113), kind=kLoop, calls=%fused_computation.3 | loop fusion | flops 11206656 | bytes 16515072 | tf_op jit(solution)/shard_map/reduce_sum | solution.py:56
  190.2 2.0 reduce_sum.63
  192.2 2.9 reshape_squeeze.10
  195.0 0.9 reduce_sum.64
  196.0 1.1 slice.123
  197.9 4.9 %collective-permute-start.6 = (bf16[5,1,8,8,192]{4,3,2,1,0:T(8,128)(2,1)S(1)}, bf16[5,1,8,8,192]{4,3,2,1,0:T(8,128)(2,1)S(1)}, u32[]{:S(2)}, u32[]{:S(2)}) collective-permute-start(bf16[5,1,8,8,192]{4,3,2,1,0:T(8,128)(2,1)S(1)} %get-tuple-element.14), channel_id=1, source_target_pairs={{0,1},{1,2},{2,3},{4,5},{5,6},{6,7},{8,9},{9,10},{10,11},{12,13},{... | collective-permute-start | bytes 368648 | tf_op jit(solution)/shard_map/ppermute | solution.py:25
  202.8 1.3 collective-permute-start.7
  204.1 6.7 %fusion.35 = f32[8,8,192]{2,1,0:T(8,128)S(1)} fusion(bf16[8,13,192,192]{3,2,0,1:T(8,128)(2,1)} %get-tuple-element.11, bf16[8,13,8,192]{3,2,1,0:T(8,128)(2,1)} %bitcast.124, pred[8,13]{1,0:T(8,128)(4,1)S(1)} %compare_and_fusion, bf16[8,8,192]{2,1,0:T(8,128)(2,1)} %copy-done.4, f32[8,192]{1,0:T(8,128)} %reduce_sum.64), kind=kOutput, calls=%fused_computation.34 | convolution fusion | flops 61538304 | bytes 8067176 | tf_op jit(solution)/shard_map/bsij,bslj->bli/dot_general | solution.py:98
  210.9 1.3 multiply_reduce_fusion.2
  212.1 42.7 %all-reduce.2 = (f32[8]{0:T(128)S(1)}, f32[8]{0:T(128)S(1)}) all-reduce(f32[8]{0:T(128)S(1)} %get-tuple-element.4, f32[8]{0:T(128)S(1)} %get-tuple-element.3), channel_id=1, replica_groups=mesh['gx'=8,'gy'=4] {'gx','gy'}, use_global_device_ids=true, to_apply=%region_2.0 | all-reduce | flops 16 | bytes 128 | tf_op jit(solution)/shard_map/psum | solution.py:84
  254.9 1.4 fusion.81
  256.7 40.5 %psum.45 = f32[8,512]{1,0:T(8,128)S(1)} all-reduce(f32[8,512]{1,0:T(8,128)S(1)} %fusion.82), channel_id=1, replica_groups=mesh['gx'=8,'gy'=4] {'gx','gy'}, use_global_device_ids=true, to_apply=%region_8.10 | all-reduce | flops 4096 | bytes 32768 | tf_op jit(solution)/shard_map/psum | solution.py:82
  297.8 39.9 %psum.46 = f32[8]{0:T(128)S(1)} all-reduce(f32[8]{0:T(128)S(1)} %get-tuple-element.24), channel_id=1, replica_groups=mesh['gx'=8,'gy'=4] {'gx','gy'}, use_global_device_ids=true, to_apply=%region_10.12 | all-reduce | flops 8 | bytes 64 | tf_op jit(solution)/shard_map/psum | solution.py:84
  337.7 4.2 collective-permute-start.8
  341.9 1.3 collective-permute-start.9
  343.5 4.2 collective-permute-done.9
  347.7 1.3 collective-permute-start.10
  349.0 1.3 collective-permute-start.11
  350.3 3.9 collective-permute-done.11
  355.0 4.8 %fusion.18 = f32[8,13,8,192]{3,2,1,0:T(8,128)S(1)} fusion(bf16[8,13,192,192]{3,2,0,1:T(8,128)(2,1)} %get-tuple-element.11, f32[8,13,192]{2,1,0:T(8,128)S(1)} %copy.49, bf16[8,13,8,192]{3,2,1,0:T(8,128)(2,1)S(1)} %bitcast.125, pred[8,13]{1,0:T(8,128)(4,1)S(1)} %compare_and_fusion, bf16[8,8,192]{2,1,0:T(8,128)(2,1)S(1)} %fusion.74), kind=kOutput, calls=%fused_computation.23 | convolution fusion | flops 61980672 | bytes 8730728 | tf_op jit(solution)/shard_map/bsij,bli->bslj/dot_general | solution.py:101
  360.8 2.9 collective-permute-start.12
  363.8 1.3 collective-permute-start.13
  366.0 4.3 %collective-permute-done.13 = bf16[1,3,8,8,192]{4,3,2,1,0:T(8,128)(2,1)S(1)} collective-permute-done((bf16[1,3,8,8,192]{4,3,2,1,0:T(8,128)(2,1)S(1)}, bf16[1,3,8,8,192]{4,3,2,1,0:T(8,128)(2,1)S(1)}, u32[]{:S(2)}, u32[]{:S(2)}) %collective-permute-start.13) | collective-permute-done | bytes 73760 | tf_op jit(solution)/shard_map/ppermute | solution.py:26
  370.4 3.7 collective-permute-start.14
  374.1 1.3 collective-permute-start.15
  375.4 5.5 %fusion.32 = f32[8,8,192]{2,1,0:T(8,128)S(1)} fusion(bf16[8,13,192,192]{3,2,0,1:T(8,128)(2,1)} %get-tuple-element.11, bf16[8,13,8,192]{3,2,1,0:T(8,128)(2,1)S(1)} %bitcast.126, pred[8,13]{1,0:T(8,128)(4,1)S(1)} %compare_and_fusion, bf16[8,8,192]{2,1,0:T(8,128)(2,1)S(1)} %fusion.74, f32[8,192]{1,0:T(8,128)S(1)} %copy-done.8), kind=kOutput, calls=%fused_computation.33 | convolution fusion | flops 61538304 | bytes 8067176 | tf_op jit(solution)/shard_map/bsij,bslj->bli/dot_general | solution.py:98
  381.3 42.7 %psum.47 = f32[8]{0:T(128)S(1)} all-reduce(f32[8]{0:T(128)S(1)} %get-tuple-element.7), channel_id=1, replica_groups=mesh['gx'=8,'gy'=4] {'gx','gy'}, use_global_device_ids=true, to_apply=%region_12.14 | all-reduce | flops 8 | bytes 64 | tf_op jit(solution)/shard_map/psum | solution.py:126
  (69 shorter events, 12.6 us)
Async XLA Ops:
  0.6 0.9 copy-start
  50.9 113.1 %copy-start.4 = (bf16[8,8,192]{2,1,0:T(8,128)(2,1)}, bf16[8,8,192]{2,1,0:T(8,128)(2,1)S(1)}, u32[]{:S(2)}) copy-start(bf16[8,8,192]{2,1,0:T(8,128)(2,1)S(1)} %get-tuple-element.22) | copy-start | bytes 73732
  51.0 104.8 %collective-permute-start = (bf16[1,1,8,8,192]{4,3,2,1,0:T(8,128)(2,1)S(1)}, bf16[1,1,8,8,192]{4,3,2,1,0:T(8,128)(2,1)S(1)}, u32[]{:S(2)}, u32[]{:S(2)}) collective-permute-start(bf16[1,1,8,8,192]{4,3,2,1,0:T(8,128)(2,1)S(1)} %bitcast.127), channel_id=1, source_target_pairs={{0,4},{4,8},{8,12},{12,16},{16,20},{20,24},{24,28},{1,5},{5,9},{9,... | collective-permute-start | bytes 73736 | tf_op jit(solution)/shard_map/ppermute | solution.py:25
  55.2 100.6 %collective-permute-start.1 = (bf16[1,1,8,8,192]{4,3,2,1,0:T(8,128)(2,1)S(1)}, bf16[1,1,8,8,192]{4,3,2,1,0:T(8,128)(2,1)}, u32[]{:S(2)}, u32[]{:S(2)}) collective-permute-start(bf16[1,1,8,8,192]{4,3,2,1,0:T(8,128)(2,1)S(1)} %bitcast.128), channel_id=1, source_target_pairs={{4,0},{8,4},{12,8},{16,12},{20,16},{24,20},{28,24},{5,1},{9,5},{13... | collective-permute-start | bytes 73736 | tf_op jit(solution)/shard_map/ppermute | solution.py:26
  121.8 14.1 %copy-start.7 = (s32[1,1,8,13]{3,2,1,0:T(8,128)S(1)}, s32[1,1,8,13]{3,2,1,0:T(8,128)}, u32[]{:S(2)}) copy-start(s32[1,1,8,13]{3,2,1,0:T(8,128)} %param.13) | copy-start | bytes 1252
  156.6 2.6 collective-permute-start.2
  157.9 4.0 collective-permute-start.3
  170.5 7.8 %copy-start.2 = (bf16[3,3,10,8,192]{4,3,2,1,0:T(8,128)(2,1)}, bf16[3,3,10,8,192]{4,3,2,1,0:T(8,128)(2,1)S(1)}, u32[]{:S(2)}) copy-start(bf16[3,3,10,8,192]{4,3,2,1,0:T(8,128)(2,1)S(1)} %reshape.65) | copy-start | bytes 829444
  171.2 25.8 %collective-permute-start.4 = (bf16[1,3,8,8,192]{4,3,2,1,0:T(8,128)(2,1)}, bf16[1,3,8,8,192]{4,3,2,1,0:T(8,128)(2,1)}, u32[]{:S(2)}, u32[]{:S(2)}) collective-permute-start(bf16[1,3,8,8,192]{4,3,2,1,0:T(8,128)(2,1)} %get-tuple-element.18), channel_id=1, source_target_pairs={{0,4},{4,8},{8,12},{12,16},{16,20},{20,24},{24,28},{1,5},{5,9},{9,... | collective-permute-start | bytes 221192 | tf_op jit(solution)/shard_map/ppermute | solution.py:25
  176.8 20.3 %collective-permute-start.5 = (bf16[1,3,8,8,192]{4,3,2,1,0:T(8,128)(2,1)}, bf16[1,3,8,8,192]{4,3,2,1,0:T(8,128)(2,1)}, u32[]{:S(2)}, u32[]{:S(2)}) collective-permute-start(bf16[1,3,8,8,192]{4,3,2,1,0:T(8,128)(2,1)} %get-tuple-element.19), channel_id=1, source_target_pairs={{4,0},{8,4},{12,8},{16,12},{20,16},{24,20},{28,24},{5,1},{9,5},{13... | collective-permute-start | bytes 221192 | tf_op jit(solution)/shard_map/ppermute | solution.py:26
  190.2 20.7 %copy-start.3 = (f32[1,1,8,8,192]{4,3,2,1,0:T(8,128)S(1)}, f32[1,1,8,8,192]{4,3,2,1,0:T(8,128)}, u32[]{:S(2)}) copy-start(f32[1,1,8,8,192]{4,3,2,1,0:T(8,128)} %param.10) | copy-start | bytes 147460
  196.0 14.9 %copy-start.1 = (bf16[8,192,192]{2,1,0:T(8,128)(2,1)S(1)}, bf16[8,192,192]{2,1,0:T(8,128)(2,1)}, u32[]{:S(2)}) copy-start(bf16[8,192,192]{2,1,0:T(8,128)(2,1)} %reshape_squeeze.10) | copy-start | bytes 1769476
  196.0 14.9 %copy-start.5 = (bf16[8,8,192]{2,1,0:T(8,128)(2,1)S(1)}, bf16[8,8,192]{2,1,0:T(8,128)(2,1)}, u32[]{:S(2)}) copy-start(bf16[8,8,192]{2,1,0:T(8,128)(2,1)} %copy-done.4) | copy-start | bytes 73732
  196.0 60.6 %copy-start.6 = (f32[16,512]{1,0:T(8,128)S(1)}, f32[16,512]{1,0:T(8,128)}, u32[]{:S(2)}) copy-start(f32[16,512]{1,0:T(8,128)} %param.17) | copy-start | bytes 98308
  197.9 12.9 %collective-permute-start.6 = (bf16[5,1,8,8,192]{4,3,2,1,0:T(8,128)(2,1)S(1)}, bf16[5,1,8,8,192]{4,3,2,1,0:T(8,128)(2,1)S(1)}, u32[]{:S(2)}, u32[]{:S(2)}) collective-permute-start(bf16[5,1,8,8,192]{4,3,2,1,0:T(8,128)(2,1)S(1)} %get-tuple-element.14), channel_id=1, source_target_pairs={{0,1},{1,2},{2,3},{4,5},{5,6},{6,7},{8,9},{9,10},{10,11},{12,13},{... | collective-permute-start | bytes 368648 | tf_op jit(solution)/shard_map/ppermute | solution.py:25
  202.8 8.0 %collective-permute-start.7 = (bf16[5,1,8,8,192]{4,3,2,1,0:T(8,128)(2,1)S(1)}, bf16[5,1,8,8,192]{4,3,2,1,0:T(8,128)(2,1)S(1)}, u32[]{:S(2)}, u32[]{:S(2)}) collective-permute-start(bf16[5,1,8,8,192]{4,3,2,1,0:T(8,128)(2,1)S(1)} %get-tuple-element.15), channel_id=1, source_target_pairs={{1,0},{2,1},{3,2},{5,4},{6,5},{7,6},{9,8},{10,9},{11,10},{13,12},{... | collective-permute-start | bytes 368648 | tf_op jit(solution)/shard_map/ppermute | solution.py:26
  297.4 78.0 %copy-start.8 = (f32[8,192]{1,0:T(8,128)S(1)}, f32[8,192]{1,0:T(8,128)}, u32[]{:S(2)}) copy-start(f32[8,192]{1,0:T(8,128)} %reduce_sum.64) | copy-start | bytes 18436
  337.7 5.8 %collective-permute-start.8 = (bf16[1,1,8,8,192]{4,3,2,1,0:T(8,128)(2,1)S(1)}, bf16[1,1,8,8,192]{4,3,2,1,0:T(8,128)(2,1)S(1)}, u32[]{:S(2)}, u32[]{:S(2)}) collective-permute-start(bf16[1,1,8,8,192]{4,3,2,1,0:T(8,128)(2,1)S(1)} %bitcast.131), channel_id=1, source_target_pairs={{0,4},{4,8},{8,12},{12,16},{16,20},{20,24},{24,28},{1,5},{5,9},{9,... | collective-permute-start | bytes 73736 | tf_op jit(solution)/shard_map/ppermute | solution.py:25
  341.9 5.8 %collective-permute-start.9 = (bf16[1,1,8,8,192]{4,3,2,1,0:T(8,128)(2,1)S(1)}, bf16[1,1,8,8,192]{4,3,2,1,0:T(8,128)(2,1)S(1)}, u32[]{:S(2)}, u32[]{:S(2)}) collective-permute-start(bf16[1,1,8,8,192]{4,3,2,1,0:T(8,128)(2,1)S(1)} %bitcast.132), channel_id=1, source_target_pairs={{4,0},{8,4},{12,8},{16,12},{20,16},{24,20},{28,24},{5,1},{9,5},{13... | collective-permute-start | bytes 73736 | tf_op jit(solution)/shard_map/ppermute | solution.py:26
  347.7 2.6 collective-permute-start.10
  349.0 5.2 %collective-permute-start.11 = (bf16[3,1,8,8,192]{4,3,2,1,0:T(8,128)(2,1)S(1)}, bf16[3,1,8,8,192]{4,3,2,1,0:T(8,128)(2,1)S(1)}, u32[]{:S(2)}, u32[]{:S(2)}) collective-permute-start(bf16[3,1,8,8,192]{4,3,2,1,0:T(8,128)(2,1)S(1)} %pad_maximum_fusion.7), channel_id=1, source_target_pairs={{1,0},{2,1},{3,2},{5,4},{6,5},{7,6},{9,8},{10,9},{11,10},{13,12},{... | collective-permute-start | bytes 221192 | tf_op jit(solution)/shard_map/ppermute | solution.py:26
  360.8 5.1 %collective-permute-start.12 = (bf16[1,3,8,8,192]{4,3,2,1,0:T(8,128)(2,1)S(1)}, bf16[1,3,8,8,192]{4,3,2,1,0:T(8,128)(2,1)S(1)}, u32[]{:S(2)}, u32[]{:S(2)}) collective-permute-start(bf16[1,3,8,8,192]{4,3,2,1,0:T(8,128)(2,1)S(1)} %get-tuple-element.16), channel_id=1, source_target_pairs={{0,4},{4,8},{8,12},{12,16},{16,20},{20,24},{24,28},{1,5},{5,9},{9,... | collective-permute-start | bytes 221192 | tf_op jit(solution)/shard_map/ppermute | solution.py:25
  363.8 6.5 %collective-permute-start.13 = (bf16[1,3,8,8,192]{4,3,2,1,0:T(8,128)(2,1)S(1)}, bf16[1,3,8,8,192]{4,3,2,1,0:T(8,128)(2,1)S(1)}, u32[]{:S(2)}, u32[]{:S(2)}) collective-permute-start(bf16[1,3,8,8,192]{4,3,2,1,0:T(8,128)(2,1)S(1)} %get-tuple-element.17), channel_id=1, source_target_pairs={{4,0},{8,4},{12,8},{16,12},{20,16},{24,20},{28,24},{5,1},{9,5},{13... | collective-permute-start | bytes 221192 | tf_op jit(solution)/shard_map/ppermute | solution.py:26
  370.4 10.5 %collective-permute-start.14 = (bf16[5,1,8,8,192]{4,3,2,1,0:T(8,128)(2,1)S(1)}, bf16[5,1,8,8,192]{4,3,2,1,0:T(8,128)(2,1)S(1)}, u32[]{:S(2)}, u32[]{:S(2)}) collective-permute-start(bf16[5,1,8,8,192]{4,3,2,1,0:T(8,128)(2,1)S(1)} %get-tuple-element.12), channel_id=1, source_target_pairs={{0,1},{1,2},{2,3},{4,5},{5,6},{6,7},{8,9},{9,10},{10,11},{12,13},{... | collective-permute-start | bytes 368648 | tf_op jit(solution)/shard_map/ppermute | solution.py:25
  374.1 6.8 %collective-permute-start.15 = (bf16[5,1,8,8,192]{4,3,2,1,0:T(8,128)(2,1)S(1)}, bf16[5,1,8,8,192]{4,3,2,1,0:T(8,128)(2,1)S(1)}, u32[]{:S(2)}, u32[]{:S(2)}) collective-permute-start(bf16[5,1,8,8,192]{4,3,2,1,0:T(8,128)(2,1)S(1)} %get-tuple-element.13), channel_id=1, source_target_pairs={{1,0},{2,1},{3,2},{5,4},{6,5},{7,6},{9,8},{10,9},{11,10},{13,12},{... | collective-permute-start | bytes 368648 | tf_op jit(solution)/shard_map/ppermute | solution.py:26
where the time goes:
time: 428 us; the launch traced here: 425 us
  blocking collectives  208 us (49%)
  local copies, waits for them, and re-layouts  95.8 us (22%)
  starting transfers between devices  38.6 us (9%)
  other arithmetic  32.7 us (8%)
  matrix products  32.5 us (8%)
  waiting for transfers between devices  16.3 us (4%)
    psum x2, blocking collectives, precondition(): summed = lax.psum(coarse_term, ('gx', 'gy'))  82.6 us
    psum x2, blocking collectives, precondition(): energy = lax.psum(jnp.sum(residual * smoothed, axis=(0, 2)), ('gx', 'gy'))  82.6 us
    mul x3, local copies, waits for them, and re-layouts, masked_blocks(): masked = shaped * intact[..., None, :, None, :]  63.1 us
    psum x1, blocking collectives, per_device(): lax.psum(jnp.sum(direction * operator_out, axis=(0, 2)), ('gx', 'gy'))  42.7 us
    ppermute x8, starting transfers between devices, padded_2(): before = lax.ppermute(last, axis, up)  28.1 us
    another operation x1, local copies, waits for them, and re-layouts, masked_blocks(): shaped = stiffness.reshape(leading + (COMP, PB, COMP, PB))  16.7 us
    ppermute x8, waiting for transfers between devices, padded_2(): after = lax.ppermute(initial, axis, down)  15.1 us
    reduce_sum x1, other arithmetic, per_device(): column_total = jnp.sum(weights, axis=2, dtype=jnp.float32)  14.1 us
  transfers between devices with their start and end apart: 16, of which 6 were waited for; matrix products, arithmetic and copies ran while one was open for 31% of the time, Pallas kernels for 0%

commit v1 on v0

v1 whole, which is shorter than its diff:
```python
import functools

import jax
import jax.numpy as jnp
from jax import lax
from jax.experimental import pallas as pl
from jax.experimental.pallas import tpu as pltpu
from jax.sharding import PartitionSpec as P

DOF = 192
HALF = 96
PAIR = 384
NS = 13
BZ = 8
NLOAD = 8
ROWS = BZ * NLOAD
ITERS = 2
SPAN = BZ + 2
GHOSTS = 9 * SPAN
SLOTS = NS + 1
HI = lax.Precision.HIGHEST
F32 = jnp.float32
BF16 = jnp.bfloat16
MESH = pl.DeviceIdType.MESH


def iota(shape, axis):
    return lax.broadcasted_iota(jnp.int32, shape, axis)


def dot(a, b, precision=None):
    return lax.dot_general(
        a, b, (((1,), (0,)), ((), ())), precision=precision, preferred_element_type=F32
    )


def dot_t(a, b, precision=None):
    return lax.dot_general(
        a, b, (((1,), (1,)), ((), ())), precision=precision, preferred_element_type=F32
    )


def prepare_kernel(bond, flags, self_flat, inv_flat, w_out, col_out, row_out, self_out, inv_out, scr):
    step = pl.program_id(0)

    def spread(read):
        @pl.loop(0, 36)
        def _(k8):
            for u in range(8):
                k = k8 * 8 + u
                scr[pl.ds(pl.multiple_of(k * 8, 8), 8), :] = read(pl.ds(pl.multiple_of(k * 128, 128), 128))

    @pl.when(step == 0)
    def _():
        row_out[...] = jnp.zeros_like(row_out)
        spread(lambda lanes: inv_flat[:, lanes])
        for z in range(BZ):
            for t in range(3):
                inv_out[z, :, t * 128 : (t + 1) * 128] = scr[pl.ds(t * 8 + z, HALF, stride=24), :]
        spread(lambda lanes: self_flat[:, lanes].astype(F32))
        for z in range(BZ):
            for t in range(3):
                self_out[z, :, t * 128 : (t + 1) * 128] = scr[
                    pl.ds(t * 8 + z, HALF, stride=24), :
                ].astype(BF16)

    spread(lambda lanes: bond[0, :, lanes].astype(F32))
    lane = iota((16, PAIR), 1)
    column = lane % DOF % 64
    code = (lane // DOF) * 8 + (column // 16) * 2 + (column % 16) // 8
    picker = (code == iota((16, PAIR), 0)).astype(BF16)
    picked = dot(flags[0], picker).astype(jnp.int32)
    lane_bit = jnp.left_shift(1, iota((1, PAIR), 1) % DOF % 8)
    keep = jnp.where((picked & lane_bit) != 0, 1.0, 0.0).astype(F32)
    for z in range(BZ):
        for t in range(3):
            lanes = slice(t * 128, (t + 1) * 128)
            mask = keep[z * 32 : (z + 1) * 32, lanes]
            part = scr[pl.ds(t * 8 + z, HALF, stride=24), :] * jnp.concatenate([mask] * 3, axis=0)
            w_out[z, :, lanes] = part.astype(BF16)
            row_out[z, :, lanes] += part
            col_out[0, z : z + 1, lanes] = jnp.sum(part, axis=0, keepdims=True)


def prepare(bond, flags, self_flat, inv_flat):
    whole = lambda *shape: pl.BlockSpec(shape, lambda s: (0,) * len(shape))
    return pl.pallas_call(
        prepare_kernel,
        grid=(NS,),
        in_specs=[
            pl.BlockSpec((1, BZ, DOF * DOF), lambda s: (s, 0, 0)),
            pl.BlockSpec((1, 256, 16), lambda s: (s, 0, 0)),
            whole(BZ, DOF * DOF),
            whole(BZ, DOF * DOF),
        ],
        out_specs=[
            pl.BlockSpec((BZ, HALF, PAIR), lambda s: (0, 0, s)),
            pl.BlockSpec((1, BZ, PAIR), lambda s: (s, 0, 0)),
            whole(BZ, HALF, PAIR),
            whole(BZ, HALF, PAIR),
            whole(BZ, HALF, PAIR),
        ],
        out_shape=[
            jax.ShapeDtypeStruct((BZ, HALF, NS * PAIR), BF16),
            jax.ShapeDtypeStruct((NS, BZ, PAIR), F32),
            jax.ShapeDtypeStruct((BZ, HALF, PAIR), F32),
            jax.ShapeDtypeStruct((BZ, HALF, PAIR), BF16),
            jax.ShapeDtypeStruct((BZ, HALF, PAIR), F32),
        ],
        scratch_shapes=[pltpu.VMEM((288 * 8, 128), F32)],
        compiler_params=pltpu.CompilerParams(vmem_limit_bytes=40 * 1024 * 1024),
        name="prepare",
    )(bond, flags, self_flat, inv_flat)


def main_kernel(
    nx,
    ny,
    codes,
    pool_at,
    load,
    w_hbm,
    col_in,
    row_in,
    self_in,
    inv_in,
    basis,
    factor,
    disp_out,
    res_out,
    w,
    col,
    row_sum,
    ghost,
    wide,
    lhs,
    terms,
    back_send,
    back_recv,
    sum_y,
    sum_x,
    image,
    even_img,
    odd_img,
    w_sem,
    halo_send_sem,
    halo_recv_sem,
    back_send_sem,
    back_recv_sem,
    y_send_sem,
    y_recv_sem,
    x_send_sem,
    x_recv_sem,
):
    cv = factor.shape[1]
    me_x, me_y = lax.axis_index("gx"), lax.axis_index("gy")

    def neighbour(n):
        x, y = me_x + n // 3 - 1, me_y + n % 3 - 1
        return x, y, (x >= 0) & (x < nx) & (y >= 0) & (y < ny)

    others = [n for n in range(9) if n != 4]
    load_w = pltpu.make_async_copy(w_hbm, w, w_sem)
    load_w.start()
    barrier = pltpu.get_barrier_semaphore()
    for n in others:
        x, y, there = neighbour(n)

        @pl.when(there)
        def _():
            pl.semaphore_signal(barrier, inc=1, device_id=(x, y), device_id_type=MESH)

    for off in range(1, ny):
        pl.semaphore_signal(
            barrier, inc=1, device_id=(me_x, lax.rem(me_y + off, ny)), device_id_type=MESH
        )
    for off in range(1, nx):
        pl.semaphore_signal(
            barrier, inc=1, device_id=(lax.rem(me_x + off, nx), me_y), device_id_type=MESH
        )

    def wait_barrier():
        peers = nx + ny - 2
        for n in others:
            peers = peers + neighbour(n)[2].astype(jnp.int32)
        pl.semaphore_wait(barrier, peers)

    to_even = (iota((DOF, HALF), 0) == 2 * iota((DOF, HALF), 1)).astype(F32)
    to_odd = (iota((DOF, HALF), 0) == 2 * iota((DOF, HALF), 1) + 1).astype(F32)
    from_even = (iota((HALF, DOF), 1) == 2 * iota((HALF, DOF), 0)).astype(F32)
    from_odd = (iota((HALF, DOF), 1) == 2 * iota((HALF, DOF), 0) + 1).astype(F32)
    lane = iota((NLOAD, 128), 1)

    def per_load(product):
        total = jnp.sum(product.reshape(BZ, NLOAD, DOF), axis=0)
        return jnp.sum(total, axis=1, keepdims=True)

    def smooth(field):
        even, odd = dot(field, to_even, HI), dot(field, to_odd, HI)
        out = []
        for z in range(BZ):
            rows = slice(z * NLOAD, (z + 1) * NLOAD)
            both = jnp.concatenate([even[rows], odd[rows]], axis=0)
            product = dot(both, inv_in[z], HI)
            out.append((product[:NLOAD] + pltpu.roll(product[NLOAD:], DOF, 1))[:, :DOF])
        return jnp.concatenate(out, axis=0)

    def restrict(field):
        total = None
        for z in range(BZ):
            part = dot_t(field[z * NLOAD : (z + 1) * NLOAD], basis[z], HI)
            total = part if total is None else total + part
        return dot(total, factor[...], HI)

    def prolong(t):
        spread = dot_t(t, factor[...], HI)
        return jnp.concatenate([dot(spread, basis[z], HI) for z in range(BZ)], axis=0)

    def pack(values):
        out = jnp.zeros((NLOAD, 128), F32)
        for k, value in enumerate(values):
            out = jnp.where(lane == k, value, out)
        return out

    def pick(packed, k):
        return jnp.sum(jnp.where(lane == k, packed, 0.0), axis=1, keepdims=True)

    def all_sum(turn, width):
        for buf, send_sem, recv_sem, me, size, axis in (
            (sum_y, y_send_sem, y_recv_sem, me_y, ny, 1),
            (sum_x, x_send_sem, x_recv_sem, me_x, nx, 0),
        ):
            copies = []
            for off in range(1, size):
                to = lax.rem(me + off, size)
                slot = buf.at[turn, me, :, pl.ds(0, width)]
                copy = pltpu.make_async_remote_copy(
                    src_ref=slot,
                    dst_ref=slot,
                    send_sem=send_sem.at[turn, off - 1],
                    recv_sem=recv_sem.at[turn, off - 1],
                    device_id=(me_x, to) if axis == 1 else (to, me_y),
                    device_id_type=MESH,
                )
                copy.start()
                copies.append(copy)
            for copy in copies:
                copy.wait_recv()
            for copy in copies:
                copy.wait_send()
            total = buf[turn, 0, :, :width]
            for j in range(1, size):
                total = total + buf[turn, j, :, :width]
            if axis == 1:
                sum_x[turn, me_x, :, :width] = total
        return total

    def exchange(turn, src, dst, send_sem, recv_sem):
        def copy_to(n):
            x, y, there = neighbour(n)
            copy = pltpu.make_async_remote_copy(
                src_ref=src(n),
                dst_ref=dst.at[turn, 8 - n],
                send_sem=send_sem.at[turn, n],
                recv_sem=recv_sem.at[turn, 8 - n],
                device_id=(x, y),
                device_id_type=MESH,
            )
            return copy, there

        def start(n):
            copy, there = copy_to(n)
            pl.when(there)(copy.start)

        def finish_recv(n):
            x, y, there = neighbour(n)
            arriving = pltpu.make_async_remote_copy(
                src_ref=src(n),
                dst_ref=dst.at[turn, n],
                send_sem=send_sem.at[turn, n],
                recv_sem=recv_sem.at[turn, n],
                device_id=(x, y),
                device_id_type=MESH,
            )
            pl.when(there)(arriving.wait_recv)

        def finish_send(n):
            copy, there = copy_to(n)
            pl.when(there)(copy.wait_send)

        return start, finish_recv, finish_send

    residual = load[...]
    smoothed = smooth(residual)
    wait_barrier()
    sum_y[0, me_y, :, :cv] = restrict(residual)
    sum_y[0, me_y, :, cv : cv + 128] = pack([per_load(residual * smoothed)])

    for turn in range(ITERS):
        for n in others:

            @pl.when(jnp.logical_not(neighbour(n)[2]))
            def _():
                ghost[turn, n] = jnp.zeros((ROWS, DOF), BF16)
                back_recv[turn, n] = jnp.zeros((ROWS, DOF), BF16)

    for n in range(9):
        wide[n * SPAN] = jnp.zeros((16, PAIR), F32)
        wide[n * SPAN + SPAN - 1] = jnp.zeros((16, PAIR), F32)
    for z in range(BZ):
        terms[z * SLOTS + NS] = jnp.zeros((NLOAD, DOF), F32)
    ones = ((iota((16, PAIR), 1) < DOF) == (iota((16, PAIR), 0) < NLOAD)).astype(F32)
    for z in range(BZ):
        row_sum[z] = dot_t(ones, row_in[z], HI)
    for s in range(NS):
        both = col_in[s]
        col[s] = (both + pltpu.roll(both, DOF, 1))[:, :DOF]

    summed = all_sum(0, cv + 128)
    coarse = summed[:, :cv]
    local_energy = pick(summed[:, cv:], 0)
    energy = local_energy + jnp.sum(coarse * coarse, axis=1, keepdims=True)
    direction = smoothed + prolong(coarse)
    shift = (iota((DOF, PAIR), 1) == iota((DOF, PAIR), 0) + DOF).astype(BF16)
    stay = (iota((DOF, PAIR), 1) == iota((DOF, PAIR), 0)).astype(BF16)

    def tiled(value):
        return jnp.concatenate([value] * BZ, axis=0)

    def apply_operator(turn, rounded):
        ghost[turn, 4] = rounded
        start, finish_recv, finish_send = exchange(
            turn, lambda n: ghost.at[turn, 4], ghost, halo_send_sem, halo_recv_sem
        )
        for n in others:
            start(n)
        even = dot(rounded, to_even.astype(BF16))
        odd = dot(rounded, to_odd.astype(BF16))
        even_img[...] = even
        odd_img[...] = odd
        if turn == 0:
            load_w.wait()

        @pl.loop(0, BZ)
        def _(z):
            rows = pl.ds(pl.multiple_of(z * NLOAD, NLOAD), NLOAD)
            both = jnp.concatenate([even_img[rows, :], odd_img[rows, :]], axis=0).astype(BF16)
            product = dot(both, w[z])
            for s in range(NS):
                part = product[:, s * PAIR : (s + 1) * PAIR]
                terms[z * SLOTS + s] = (part[:NLOAD] + pltpu.roll(part[NLOAD:], DOF, 1))[:, :DOF]

        for n in others:
            finish_recv(n)

        @pl.loop(0, 9)
        def _(n):
            field = ghost[turn, n]
            top, bottom = dot(field, stay), dot(field, shift)
            for z in range(BZ):
                rows = slice(z * NLOAD, (z + 1) * NLOAD)
                wide[n * SPAN + 1 + z, :NLOAD, :] = top[rows]
                wide[n * SPAN + 1 + z, NLOAD:, :] = bottom[rows]

        @pl.loop(0, BZ)
        def _(z):
            for s in range(NS):
                at = codes[z * NS + s]
                near = wide[at]
                lhs[z, :, s * PAIR : (s + 1) * PAIR] = near.astype(BF16)
                terms[z * SLOTS + s] = (
                    col[s, pl.ds(z, 1), :] * near[:NLOAD, :DOF] - terms[z * SLOTS + s]
                )

        def pooled(n, z):
            total = None
            for b in range(3):
                part = terms[pool_at[(n * BZ + z) * 3 + b]]
                total = part if total is None else total + part
            return total

        start, finish_back, finish_back_send = exchange(
            turn, lambda n: back_send.at[turn, n], back_recv, back_send_sem, back_recv_sem
        )
        for n in others:

            @pl.loop(0, BZ // 2)
            def _(z2):
                both = jnp.concatenate([pooled(n, z2 * 2), pooled(n, z2 * 2 + 1)], axis=0)
                back_send[turn, n, pl.ds(pl.multiple_of(z2 * 16, 16), 16), :] = both.astype(BF16)

            start(n)

        @pl.loop(0, BZ)
        def _(z):
            rows = pl.ds(pl.multiple_of(z * NLOAD, NLOAD), NLOAD)
            own = wide[4 * SPAN + 1 + z].astype(BF16)
            out = dot_t(own, self_in[z]) - dot_t(lhs[z], w[z])
            both = jnp.concatenate([even_img[rows, :], odd_img[rows, :]], axis=0)
            out = out + row_sum[z] * both
            even_img[rows, :] = out[:NLOAD]
            odd_img[rows, :] = out[NLOAD:]
            image[rows, :] = pooled(4, z)

        out = image[...] + dot(even_img[...], from_even, HI) + dot(odd_img[...], from_odd, HI)
        for n in others:
            finish_back(n)
            out = out + back_recv[turn, n].astype(F32)
        for n in others:
            finish_send(n)
            finish_back_send(n)
        return out

    out = apply_operator(0, direction.astype(BF16))
    smooth_out = smooth(out)
    sum_y[1, me_y, :, :cv] = restrict(out)
    sum_y[1, me_y, :, cv : cv + 128] = pack(
        [
            per_load(direction * out),
            per_load(residual * smooth_out + out * smoothed),
            per_load(out * smooth_out),
        ]
    )
    summed = all_sum(1, cv + 128)
    scalars = summed[:, cv:]
    step = energy / pick(scalars, 0)
    coarse = coarse - step * summed[:, :cv]
    local_energy = local_energy - step * pick(scalars, 1) + step * step * pick(scalars, 2)
    new_energy = local_energy + jnp.sum(coarse * coarse, axis=1, keepdims=True)
    step_all = tiled(step)
    moved = step_all * direction
    residual = residual - step_all * out
    smoothed = smoothed - step_all * smooth_out
    direction = smoothed + prolong(coarse) + tiled(new_energy / energy) * direction

    out = apply_operator(1, direction.astype(BF16))
    sum_y[2, me_y, :, :128] = pack([per_load(direction * out)])
    step_all = tiled(new_energy / pick(all_sum(2, 128), 0))
    disp_out[...] = moved + step_all * direction
    res_out[...] = residual - step_all * out


def per_device(load, bond, words, block_cols, self_flat, inv_flat, basis, factor):
    nx, ny = lax.axis_size("gx"), lax.axis_size("gy")
    cv = factor.shape[1]
    words = words[0, 0]
    both = jnp.stack([words & 255, words >> 8], axis=-1)
    flags = (
        both.reshape(BZ, NS, 32, 16).transpose(1, 0, 2, 3).reshape(NS, 256, 16).astype(BF16)
    )
    codes = block_cols[0, 0]
    z = jnp.arange(BZ, dtype=jnp.int32)[:, None]
    offset = (codes // SPAN) * 3 + codes % SPAN - z
    hit = offset[:, :, None] == jnp.arange(27, dtype=jnp.int32)
    slot = jnp.sum(jnp.where(hit, jnp.arange(NS, dtype=jnp.int32)[:, None] - NS, 0), axis=1) + NS
    table = jnp.pad((slot + z * SLOTS).reshape(BZ, 9, 3), ((1, 1), (0, 0), (0, 0)), constant_values=NS)
    pool_at = jnp.stack([table[2 - b : 2 - b + BZ, :, b] for b in range(3)], axis=-1)
    pool_at = pool_at.transpose(1, 0, 2).reshape(-1)

    w, col, row, self_pairs, inv_pairs = prepare(
        bond[0, 0].transpose(1, 0, 2), flags, self_flat[0, 0], inv_flat[0, 0]
    )
    vmem = pl.BlockSpec(memory_space=pltpu.VMEM)
    smem = pl.BlockSpec(memory_space=pltpu.SMEM)
    dma = pltpu.SemaphoreType.DMA
    disp, res = pl.pallas_call(
        functools.partial(main_kernel, nx, ny),
        in_specs=[smem, smem, vmem, pl.BlockSpec(memory_space=pl.ANY)] + [vmem] * 6,
        out_specs=[vmem, vmem],
        out_shape=[jax.ShapeDtypeStruct((ROWS, DOF), F32)] * 2,
        scratch_shapes=[
            pltpu.VMEM((BZ, HALF, NS * PAIR), BF16),
            pltpu.VMEM((NS, BZ, DOF), F32),
            pltpu.VMEM((BZ, 16, HALF), F32),
            pltpu.VMEM((ITERS, 9, ROWS, DOF), BF16),
            pltpu.VMEM((GHOSTS, 16, PAIR), F32),
            pltpu.VMEM((BZ, 16, NS * PAIR), BF16),
            pltpu.VMEM((BZ * SLOTS, NLOAD, DOF), F32),
            pltpu.VMEM((ITERS, 9, ROWS, DOF), BF16),
            pltpu.VMEM((ITERS, 9, ROWS, DOF), BF16),
            pltpu.VMEM((3, ny, NLOAD, cv + 128), F32),
            pltpu.VMEM((3, nx, NLOAD, cv + 128), F32),
            pltpu.VMEM((ROWS, DOF), F32),
            pltpu.VMEM((ROWS, HALF), F32),
            pltpu.VMEM((ROWS, HALF), F32),
            dma,
            dma((ITERS, 9)),
            dma((ITERS, 9)),
            dma((ITERS, 9)),
            dma((ITERS, 9)),
            dma((3, ny)),
            dma((3, ny)),
            dma((3, nx)),
            dma((3, nx)),
        ],
        compiler_params=pltpu.CompilerParams(
            collective_id=0, has_side_effects=True, vmem_limit_bytes=56 * 1024 * 1024
        ),
        name="conjugate_gradients",
    )(
        codes.reshape(-1),
        pool_at,
        load.reshape(ROWS, DOF),
        w,
        col,
        row,
        self_pairs,
        inv_pairs,
        basis[0, 0].transpose(1, 0, 2),
        factor,
    )
    shape = (1, 1, BZ, NLOAD, DOF)
    return disp.reshape(shape), res.reshape(shape)


def solution(mesh):
    in_specs = (
        P("gx", "gy", None, None, None),
        P("gx", "gy", None, None, None),
        P("gx", "gy", None, None, None, None),
        P("gx", "gy", None, None),
        P("gx", "gy", None, None),
        P("gx", "gy", None, None),
        P("gx", "gy", None, None, None),
        P(("gx", "gy"), None),
    )
    out_specs = (P("gx", "gy", None, None, None), P("gx", "gy", None, None, None))
    return jax.shard_map(
        per_device, mesh=mesh, in_specs=in_specs, out_specs=out_specs, check_vma=False
    )
```

time: 428 us -> 97.9 us (0.23)
  blocking collectives: 208 us -> 0 us
  local copies, waits for them, and re-layouts: 95.8 us -> 18.2 us
  Pallas kernels: 0 us -> 77.1 us
  starting transfers between devices: 38.6 us -> 0 us
  matrix products: 32.5 us -> 0 us
  other arithmetic: 32.7 us -> 1.35 us
  waiting for transfers between devices: 16.3 us -> 0 us
    psum x5 -> x0, blocking collectives: 208 us -> none  [the longest x2 82.6 us: precondition(): summed = lax.psum(coarse_term, ('gx', 'gy'))]
    pallas_call x0 -> x2, Pallas kernels: none -> 77.1 us  [the longest x1 60.7 us: per_device(): pl.pallas_call(functools.partial(main_kernel, nx, ny), in_specs=[smem, sm...]
    mul x3 -> x0, local copies, waits for them, and re-layouts: 63.1 us -> none  [masked_blocks(): masked = shaped * intact[..., None, :, None, :]]
    ppermute x16 -> x0, starting transfers between devices: 38.6 us -> none  [the longest x8 28.1 us: padded_2(): before = lax.ppermute(last, axis, up)]
    dot_general x20 -> x0, matrix products: 32.5 us -> none  [the longest x2 12.1 us: per_device(): jnp.einsum('bsij,bslj->bli', weights, gathered, preferred_element_type=jn...]
    reduce_sum x3 -> x1, other arithmetic: 26.9 us -> 0.1 us  [per_device(): jnp.sum(jnp.where(hit, jnp.arange(NS, dtype=jnp.int32)[:, None] - NS, 0),...]
    another operation x3 -> x2, local copies, waits for them, and re-layouts: 21.5 us -> 3.27 us  [the longest x1 2.68 us: per_device(): both = jnp.stack([words & 255, words >> 8], axis=-1)]
    ppermute x16 -> x0, waiting for transfers between devices: 16.3 us -> none  [the longest x8 15.1 us: padded_2(): after = lax.ppermute(initial, axis, down)]
  transfers between devices with their start and end apart: 16 -> 0, of which waited for: 6 -> 0; matrix products, arithmetic and copies ran while one was open for 31% -> 0% of each run, Pallas kernels for 0% -> 0%
where the time goes in v1:
time: 97.9 us; the launch traced here: 97.4 us
  Pallas kernels  77.1 us (79%)
  local copies, waits for them, and re-layouts  18.2 us (19%)
  other arithmetic  1.35 us (1%)
    pallas_call x1, Pallas kernels, per_device(): pl.pallas_call(functools.partial(main_kernel, nx, ny), in_specs=[smem, sm...  60.7 us
    pallas_call x1, Pallas kernels, prepare(): pl.pallas_call(prepare_kernel, grid=(NS,), in_specs=[pl.BlockSpec((1, BZ,...  16.3 us
    unnamed x21, local copies, waits for them, and re-layouts  10.3 us
    convert_element_type x1, local copies, waits for them, and re-layouts, per_device(): both.reshape(BZ, NS, 32, 16).transpose(1, 0, 2, 3).reshape(NS, 256, 16)  3.5 us
    another operation x1, local copies, waits for them, and re-layouts, per_device(): both = jnp.stack([words & 255, words >> 8], axis=-1)  2.68 us

profile of v1, /device:TPU:0, one launch (start us, length us, event | category | flops | bytes accessed | tf_op | source)
XLA Modules:
  0.0 97.4 jit_solution(10905573349885301100)
XLA Ops:
  0.6 1.0 %fusion = (bf16[8,13,64,4,1]{2,3,1,0,4:T(4,128)(2,1)S(1)}, bf16[8,13,64,4,1]{2,3,1,0,4:T(4,128)(2,1)S(1)}) fusion(s32[1,1,8,13,64,4]{4,5,3,2,1,0:T(4,128)} %param.10), kind=kLoop, calls=%fused_computation.4 | loop fusion | flops 106496 | bytes 212992 | tf_op jit(solution)/shard_map/and | solution.py:447
  1.7 0.2 pad_maximum_fusion
  1.8 2.7 %copy.18 = bf16[8,13,64,4,2]{1,0,4,3,2:T(8,128)(2,1)} copy(bf16[8,13,64,4,2]{2,3,1,0,4:T(4,128)(2,1)S(1)} %pad_maximum_fusion) | data formatting | bytes 212992 | tf_op jit(solution)/shard_map/stack | solution.py:447
  4.5 0.0 copy-start.1
  4.5 0.0 copy-start.4
  4.5 3.5 %copy.19 = bf16[13,8,32,16]{3,2,1,0:T(8,128)(2,1)S(1)} copy(bf16[13,8,32,16]{0,1,3,2:T(8,128)(2,1)} %bitcast.49) | data formatting | bytes 212992 | tf_op jit(solution)/shard_map/convert_element_type | solution.py:449
  8.0 0.0 copy-done.1
  8.0 0.0 copy-done.4
  8.0 0.0 copy-start.8
  8.1 0.0 copy-start.7
  8.1 16.3 %prepare.1 = (bf16[8,96,4992]{2,1,0:T(8,128)(2,1)S(1)}, f32[13,8,384]{2,1,0:T(8,128)S(1)}, f32[8,96,384]{2,1,0:T(8,128)S(1)}, bf16[8,96,384]{2,1,0:T(8,128)(2,1)S(1)}, f32[8,96,384]{2,1,0:T(8,128)S(1)}) custom-call(bf16[13,8,36864]{2,1,0:T(8,128)(2,1)} %bitcast.48, bf16[13,256,16]{2,1,0:T(8,128)(2,1)S(1)} %bitcast.45, bf16[8,36864]{1,0:T(8,128)(2,1)S(1)} %bitcast.47, ...), custom_call_target="tpu_custom_call" | custom-call | tf_op jit(solution)/shard_map/prepare/pallas_call | solution.py:87
  24.4 0.0 copy-start
  24.4 3.0 %copy-done = bf16[8,96,4992]{2,1,0:T(8,128)(2,1)} copy-done((bf16[8,96,4992]{2,1,0:T(8,128)(2,1)}, bf16[8,96,4992]{2,1,0:T(8,128)(2,1)S(1)}, u32[]{:S(2)}) %copy-start) | copy-done | bytes 7667736
  27.4 0.0 copy-start.2
  27.4 1.1 %copy-done.2 = f32[8,96,384]{2,1,0:T(8,128)} copy-done((f32[8,96,384]{2,1,0:T(8,128)}, f32[8,96,384]{2,1,0:T(8,128)S(1)}, u32[]{:S(2)}) %copy-start.2) | copy-done | bytes 1179672
  28.5 0.0 copy-start.3
  28.5 1.0 %copy-done.3 = f32[8,96,384]{2,1,0:T(8,128)} copy-done((f32[8,96,384]{2,1,0:T(8,128)}, f32[8,96,384]{2,1,0:T(8,128)S(1)}, u32[]{:S(2)}) %copy-start.3) | copy-done | bytes 1179672
  29.6 0.0 copy-start.5
  29.6 0.8 copy-done.5
  30.4 0.0 copy-start.6
  30.4 0.7 copy-done.6
  31.1 0.0 copy-done.8
  31.1 0.1 copy.15
  31.2 0.1 select_reduce_fusion
  31.3 0.1 copy.16
  31.4 0.1 pad_slice_fusion.1
  31.6 0.1 copy.17
  31.7 0.7 reshape.102.pool_at
  32.4 0.0 copy-done.7
  32.4 0.7 copy.22
  33.1 0.6 reshape_squeeze.3.codes
  33.7 60.7 %conjugate_gradients.1 = (f32[64,192]{1,0:T(8,128)}, f32[64,192]{1,0:T(8,128)}) custom-call(s32[104]{0:T(128)} %reshape_squeeze.3.codes, s32[216]{0:T(256)} %reshape.102.pool_at, f32[64,192]{1,0:T(8,128)} %bitcast.51, bf16[8,96,4992]{2,1,0:T(8,128)(2,1)} %copy-done, f32[13,8,384]{2,1,0:T(8,128)} %copy-done.6, f32[8,96,384]{2,1,0:T(8,128)} %copy-done.2, ...), custom_call_target="tpu_custom_call" | custom-call | tf_op jit(solution)/shard_map/conjugate_gradients/pallas_call | solution.py:466
  94.4 1.5 %copy.25 = f32[1,1,8,8,192]{4,3,2,1,0:T(8,128)} copy(f32[1,1,8,8,192]{4,3,2,1,0:T(8,128)} %bitcast.53) | data formatting | bytes 98304
  95.9 1.5 %copy.26 = f32[1,1,8,8,192]{4,3,2,1,0:T(8,128)} copy(f32[1,1,8,8,192]{4,3,2,1,0:T(8,128)} %bitcast.52) | data formatting | bytes 98304
  (7 shorter events, 0.1 us)
Async XLA Ops:
  4.5 3.5 %copy-start.1 = (f32[1,1,8,36864]{3,2,1,0:T(8,128)S(1)}, f32[1,1,8,36864]{3,2,1,0:T(8,128)}, u32[]{:S(2)}) copy-start(f32[1,1,8,36864]{3,2,1,0:T(8,128)} %param.13) | copy-start | bytes 3538948
  4.5 3.5 %copy-start.4 = (bf16[1,1,8,36864]{3,2,1,0:T(8,128)(2,1)S(1)}, bf16[1,1,8,36864]{3,2,1,0:T(8,128)(2,1)}, u32[]{:S(2)}) copy-start(bf16[1,1,8,36864]{3,2,1,0:T(8,128)(2,1)} %param.12) | copy-start | bytes 1769476
  8.0 23.0 %copy-start.8 = (s32[1,1,8,13]{3,2,1,0:T(8,128)S(1)}, s32[1,1,8,13]{3,2,1,0:T(8,128)}, u32[]{:S(2)}) copy-start(s32[1,1,8,13]{3,2,1,0:T(8,128)} %param.11) | copy-start | bytes 1252
  8.1 24.3 %copy-start.7 = (f32[1,1,16,8,192]{4,3,2,1,0:T(8,128)S(1)}, f32[1,1,16,8,192]{4,3,2,1,0:T(8,128)}, u32[]{:S(2)}) copy-start(f32[1,1,16,8,192]{4,3,2,1,0:T(8,128)} %param.14) | copy-start | bytes 294916
  24.4 3.0 %copy-start = (bf16[8,96,4992]{2,1,0:T(8,128)(2,1)}, bf16[8,96,4992]{2,1,0:T(8,128)(2,1)S(1)}, u32[]{:S(2)}) copy-start(bf16[8,96,4992]{2,1,0:T(8,128)(2,1)S(1)} %get-tuple-element.9.w_hbm) | copy-start | bytes 23003140
  27.4 1.1 %copy-start.2 = (f32[8,96,384]{2,1,0:T(8,128)}, f32[8,96,384]{2,1,0:T(8,128)S(1)}, u32[]{:S(2)}) copy-start(f32[8,96,384]{2,1,0:T(8,128)S(1)} %get-tuple-element.11.row_in) | copy-start | bytes 3538948
  28.5 1.0 %copy-start.3 = (f32[8,96,384]{2,1,0:T(8,128)}, f32[8,96,384]{2,1,0:T(8,128)S(1)}, u32[]{:S(2)}) copy-start(f32[8,96,384]{2,1,0:T(8,128)S(1)} %get-tuple-element.13.inv_in) | copy-start | bytes 3538948
  29.6 0.8 copy-start.5
  30.4 0.7 copy-start.6

commit v2 on v1

--- a/solution.py
+++ b/solution.py
@@ -40,7 +40,9 @@
     )
 
 
-def prepare_kernel(bond, flags, self_flat, inv_flat, w_out, col_out, row_out, self_out, inv_out, scr):
+def prepare_kernel(
+    bond, words, self_flat, inv_flat, w_out, col_out, row_out, self_out, inv_hi, inv_lo, scr, place
+):
     step = pl.program_id(0)
 
     def spread(read):
@@ -53,10 +55,16 @@
     @pl.when(step == 0)
     def _():
         row_out[...] = jnp.zeros_like(row_out)
+        point, at = iota((512, 512), 0), iota((512, 512), 1)
+        to = at % 256
+        place[...] = (point == (to // 32) * 64 + (to % 32) * 2 + at // 256).astype(BF16)
         spread(lambda lanes: inv_flat[:, lanes])
         for z in range(BZ):
             for t in range(3):
-                inv_out[z, :, t * 128 : (t + 1) * 128] = scr[pl.ds(t * 8 + z, HALF, stride=24), :]
+                value = scr[pl.ds(t * 8 + z, HALF, stride=24), :]
+                high = value.astype(BF16)
+                inv_hi[z, :, t * 128 : (t + 1) * 128] = high
+                inv_lo[z, :, t * 128 : (t + 1) * 128] = (value - high.astype(F32)).astype(BF16)
         spread(lambda lanes: self_flat[:, lanes].astype(F32))
         for z in range(BZ):
             for t in range(3):
@@ -67,9 +75,13 @@
     spread(lambda lanes: bond[0, :, lanes].astype(F32))
     lane = iota((16, PAIR), 1)
     column = lane % DOF % 64
-    code = (lane // DOF) * 8 + (column // 16) * 2 + (column % 16) // 8
+    code = (lane // DOF) * 8 + (column % 16) // 8 * 4 + column // 16
     picker = (code == iota((16, PAIR), 0)).astype(BF16)
-    picked = dot(flags[0], picker).astype(jnp.int32)
+    packed = jnp.concatenate([words[z, 0] for z in range(BZ)], axis=1)
+    halves = jnp.concatenate([packed & 255, packed >> 8], axis=0).astype(F32).astype(BF16)
+    apart = dot(halves, place[...])
+    flags = jnp.concatenate([apart[:, :256], apart[:, 256:]], axis=0).T.astype(BF16)
+    picked = dot(flags, picker).astype(jnp.int32)
     lane_bit = jnp.left_shift(1, iota((1, PAIR), 1) % DOF % 8)
     keep = jnp.where((picked & lane_bit) != 0, 1.0, 0.0).astype(F32)
     for z in range(BZ):
@@ -82,14 +94,14 @@
             col_out[0, z : z + 1, lanes] = jnp.sum(part, axis=0, keepdims=True)
 
 
-def prepare(bond, flags, self_flat, inv_flat):
+def prepare(bond, words, self_flat, inv_flat):
     whole = lambda *shape: pl.BlockSpec(shape, lambda s: (0,) * len(shape))
     return pl.pallas_call(
         prepare_kernel,
         grid=(NS,),
         in_specs=[
             pl.BlockSpec((1, BZ, DOF * DOF), lambda s: (s, 0, 0)),
-            pl.BlockSpec((1, 256, 16), lambda s: (s, 0, 0)),
+            pl.BlockSpec((BZ, 1, 4, 64), lambda s: (0, s, 0, 0)),
             whole(BZ, DOF * DOF),
             whole(BZ, DOF * DOF),
         ],
@@ -99,18 +111,20 @@
             whole(BZ, HALF, PAIR),
             whole(BZ, HALF, PAIR),
             whole(BZ, HALF, PAIR),
+            whole(BZ, HALF, PAIR),
         ],
         out_shape=[
             jax.ShapeDtypeStruct((BZ, HALF, NS * PAIR), BF16),
             jax.ShapeDtypeStruct((NS, BZ, PAIR), F32),
             jax.ShapeDtypeStruct((BZ, HALF, PAIR), F32),
             jax.ShapeDtypeStruct((BZ, HALF, PAIR), BF16),
-            jax.ShapeDtypeStruct((BZ, HALF, PAIR), F32),
+            jax.ShapeDtypeStruct((BZ, HALF, PAIR), BF16),
+            jax.ShapeDtypeStruct((BZ, HALF, PAIR), BF16),
         ],
-        scratch_shapes=[pltpu.VMEM((288 * 8, 128), F32)],
-        compiler_params=pltpu.CompilerParams(vmem_limit_bytes=40 * 1024 * 1024),
+        scratch_shapes=[pltpu.VMEM((288 * 8, 128), F32), pltpu.VMEM((512, 512), BF16)],
+        compiler_params=pltpu.CompilerParams(vmem_limit_bytes=50 * 1024 * 1024),
         name="prepare",
-    )(bond, flags, self_flat, inv_flat)
+    )(bond, words, self_flat, inv_flat)
 
 
 def main_kernel(
@@ -123,7 +137,8 @@
     col_in,
     row_in,
     self_in,
-    inv_in,
+    inv_high,
+    inv_low,
     basis,
     factor,
     disp_out,
@@ -142,6 +157,7 @@
     image,
     even_img,
     odd_img,
+    forward,
     w_sem,
     halo_send_sem,
     halo_recv_sem,
@@ -185,23 +201,30 @@
             peers = peers + neighbour(n)[2].astype(jnp.int32)
         pl.semaphore_wait(barrier, peers)
 
-    to_even = (iota((DOF, HALF), 0) == 2 * iota((DOF, HALF), 1)).astype(F32)
-    to_odd = (iota((DOF, HALF), 0) == 2 * iota((DOF, HALF), 1) + 1).astype(F32)
-    from_even = (iota((HALF, DOF), 1) == 2 * iota((HALF, DOF), 0)).astype(F32)
-    from_odd = (iota((HALF, DOF), 1) == 2 * iota((HALF, DOF), 0) + 1).astype(F32)
+    to_even = (iota((DOF, HALF), 0) == 2 * iota((DOF, HALF), 1)).astype(BF16)
+    to_odd = (iota((DOF, HALF), 0) == 2 * iota((DOF, HALF), 1) + 1).astype(BF16)
+    from_even = (iota((HALF, DOF), 1) == 2 * iota((HALF, DOF), 0)).astype(BF16)
+    from_odd = (iota((HALF, DOF), 1) == 2 * iota((HALF, DOF), 0) + 1).astype(BF16)
     lane = iota((NLOAD, 128), 1)
 
     def per_load(product):
         total = jnp.sum(product.reshape(BZ, NLOAD, DOF), axis=0)
         return jnp.sum(total, axis=1, keepdims=True)
 
+    def split(field):
+        high = field.astype(BF16)
+        return high, (field - high.astype(F32)).astype(BF16)
+
     def smooth(field):
-        even, odd = dot(field, to_even, HI), dot(field, to_odd, HI)
+        parts = jnp.concatenate(split(field), axis=0)
+        even, odd = dot(parts, to_even), dot(parts, to_odd)
         out = []
         for z in range(BZ):
-            rows = slice(z * NLOAD, (z + 1) * NLOAD)
-            both = jnp.concatenate([even[rows], odd[rows]], axis=0)
-            product = dot(both, inv_in[z], HI)
+            high = slice(z * NLOAD, (z + 1) * NLOAD)
+            low = slice(ROWS + z * NLOAD, ROWS + (z + 1) * NLOAD)
+            both = jnp.concatenate([even[high], odd[high], even[low], odd[low]], axis=0).astype(BF16)
+            first = dot(both, inv_high[z])
+            product = first[:16] + first[16:] + dot(both[:16], inv_low[z])
             out.append((product[:NLOAD] + pltpu.roll(product[NLOAD:], DOF, 1))[:, :DOF])
         return jnp.concatenate(out, axis=0)
 
@@ -225,7 +248,7 @@
     def pick(packed, k):
         return jnp.sum(jnp.where(lane == k, packed, 0.0), axis=1, keepdims=True)
 
-    def all_sum(turn, width):
+    def all_sum(turn, width, beside=lambda: None):
         for buf, send_sem, recv_sem, me, size, axis in (
             (sum_y, y_send_sem, y_recv_sem, me_y, ny, 1),
             (sum_x, x_send_sem, x_recv_sem, me_x, nx, 0),
@@ -244,6 +267,8 @@
                 )
                 copy.start()
                 copies.append(copy)
+            if axis == 1:
+                beside()
             for copy in copies:
                 copy.wait_recv()
             for copy in copies:
@@ -296,27 +321,28 @@
     sum_y[0, me_y, :, :cv] = restrict(residual)
     sum_y[0, me_y, :, cv : cv + 128] = pack([per_load(residual * smoothed)])
 
-    for turn in range(ITERS):
-        for n in others:
-
-            @pl.when(jnp.logical_not(neighbour(n)[2]))
-            def _():
-                ghost[turn, n] = jnp.zeros((ROWS, DOF), BF16)
-                back_recv[turn, n] = jnp.zeros((ROWS, DOF), BF16)
-
-    for n in range(9):
-        wide[n * SPAN] = jnp.zeros((16, PAIR), F32)
-        wide[n * SPAN + SPAN - 1] = jnp.zeros((16, PAIR), F32)
-    for z in range(BZ):
-        terms[z * SLOTS + NS] = jnp.zeros((NLOAD, DOF), F32)
-    ones = ((iota((16, PAIR), 1) < DOF) == (iota((16, PAIR), 0) < NLOAD)).astype(F32)
-    for z in range(BZ):
-        row_sum[z] = dot_t(ones, row_in[z], HI)
-    for s in range(NS):
-        both = col_in[s]
-        col[s] = (both + pltpu.roll(both, DOF, 1))[:, :DOF]
-
-    summed = all_sum(0, cv + 128)
+    def set_up():
+        for turn in range(ITERS):
+            for n in others:
+
+                @pl.when(jnp.logical_not(neighbour(n)[2]))
+                def _():
+                    ghost[turn, n] = jnp.zeros((ROWS, DOF), BF16)
+                    back_recv[turn, n] = jnp.zeros((ROWS, DOF), BF16)
+
+        for n in range(9):
+            wide[n * SPAN] = jnp.zeros((16, PAIR), F32)
+            wide[n * SPAN + SPAN - 1] = jnp.zeros((16, PAIR), F32)
+        for z in range(BZ):
+            terms[z * SLOTS + NS] = jnp.zeros((NLOAD, DOF), F32)
+        ones = ((iota((16, PAIR), 1) < DOF) == (iota((16, PAIR), 0) < NLOAD)).astype(F32)
+        sums = jnp.concatenate([dot_t(row_in[z], ones, HI) for z in range(BZ)], axis=1)
+        row_sum[...] = sums.T
+        for s in range(NS):
+            both = col_in[s]
+            col[s] = (both + pltpu.roll(both, DOF, 1))[:, :DOF]
+
+    summed = all_sum(0, cv + 128, set_up)
     coarse = summed[:, :cv]
     local_energy = pick(summed[:, cv:], 0)
     energy = local_energy + jnp.sum(coarse * coarse, axis=1, keepdims=True)
@@ -334,8 +360,8 @@
         )
         for n in others:
             start(n)
-        even = dot(rounded, to_even.astype(BF16))
-        odd = dot(rounded, to_odd.astype(BF16))
+        even = dot(rounded, to_even)
+        odd = dot(rounded, to_odd)
         even_img[...] = even
         odd_img[...] = odd
         if turn == 0:
@@ -395,14 +421,18 @@
         def _(z):
             rows = pl.ds(pl.multiple_of(z * NLOAD, NLOAD), NLOAD)
             own = wide[4 * SPAN + 1 + z].astype(BF16)
-            out = dot_t(own, self_in[z]) - dot_t(lhs[z], w[z])
-            both = jnp.concatenate([even_img[rows, :], odd_img[rows, :]], axis=0)
-            out = out + row_sum[z] * both
-            even_img[rows, :] = out[:NLOAD]
-            odd_img[rows, :] = out[NLOAD:]
+            forward[z] = dot_t(self_in[z], own) - dot_t(w[z], lhs[z])
             image[rows, :] = pooled(4, z)
 
-        out = image[...] + dot(even_img[...], from_even, HI) + dot(odd_img[...], from_odd, HI)
+        both = jnp.concatenate([forward[z] for z in range(BZ)], axis=1).T.reshape(BZ, 2, NLOAD, HALF)
+        rates = row_sum[...].reshape(BZ, 2, NLOAD, HALF)
+        out = image[...]
+        for half, source, into in ((0, even_img, from_even), (1, odd_img, from_odd)):
+            value = both[:, half].reshape(ROWS, HALF) + rates[:, half].reshape(ROWS, HALF) * source[...]
+            high, rest = split(value)
+            low = (value - high.astype(F32) - rest.astype(F32)).astype(BF16)
+            for part in (low, rest, high):
+                out = out + dot(part, into)
         for n in others:
             finish_back(n)
             out = out + back_recv[turn, n].astype(F32)
@@ -443,11 +473,6 @@
 def per_device(load, bond, words, block_cols, self_flat, inv_flat, basis, factor):
     nx, ny = lax.axis_size("gx"), lax.axis_size("gy")
     cv = factor.shape[1]
-    words = words[0, 0]
-    both = jnp.stack([words & 255, words >> 8], axis=-1)
-    flags = (
-        both.reshape(BZ, NS, 32, 16).transpose(1, 0, 2, 3).reshape(NS, 256, 16).astype(BF16)
-    )
     codes = block_cols[0, 0]
     z = jnp.arange(BZ, dtype=jnp.int32)[:, None]
     offset = (codes // SPAN) * 3 + codes % SPAN - z
@@ -457,21 +482,21 @@
     pool_at = jnp.stack([table[2 - b : 2 - b + BZ, :, b] for b in range(3)], axis=-1)
     pool_at = pool_at.transpose(1, 0, 2).reshape(-1)
 
-    w, col, row, self_pairs, inv_pairs = prepare(
-        bond[0, 0].transpose(1, 0, 2), flags, self_flat[0, 0], inv_flat[0, 0]
+    w, col, row, self_pairs, inv_high, inv_low = prepare(
+        bond[0, 0].transpose(1, 0, 2), words[0, 0].transpose(0, 1, 3, 2), self_flat[0, 0], inv_flat[0, 0]
     )
     vmem = pl.BlockSpec(memory_space=pltpu.VMEM)
     smem = pl.BlockSpec(memory_space=pltpu.SMEM)
     dma = pltpu.SemaphoreType.DMA
     disp, res = pl.pallas_call(
         functools.partial(main_kernel, nx, ny),
-        in_specs=[smem, smem, vmem, pl.BlockSpec(memory_space=pl.ANY)] + [vmem] * 6,
+        in_specs=[smem, smem, vmem, pl.BlockSpec(memory_space=pl.ANY)] + [vmem] * 7,
         out_specs=[vmem, vmem],
         out_shape=[jax.ShapeDtypeStruct((ROWS, DOF), F32)] * 2,
         scratch_shapes=[
             pltpu.VMEM((BZ, HALF, NS * PAIR), BF16),
             pltpu.VMEM((NS, BZ, DOF), F32),
-            pltpu.VMEM((BZ, 16, HALF), F32),
+            pltpu.VMEM((BZ * 16, HALF), F32),
             pltpu.VMEM((ITERS, 9, ROWS, DOF), BF16),
             pltpu.VMEM((GHOSTS, 16, PAIR), F32),
             pltpu.VMEM((BZ, 16, NS * PAIR), BF16),
@@ -483,6 +508,7 @@
             pltpu.VMEM((ROWS, DOF), F32),
             pltpu.VMEM((ROWS, HALF), F32),
             pltpu.VMEM((ROWS, HALF), F32),
+            pltpu.VMEM((BZ, HALF, 16), F32),
             dma,
             dma((ITERS, 9)),
             dma((ITERS, 9)),
@@ -494,7 +520,7 @@
             dma((3, nx)),
         ],
         compiler_params=pltpu.CompilerParams(
-            collective_id=0, has_side_effects=True, vmem_limit_bytes=56 * 1024 * 1024
+            collective_id=0, has_side_effects=True, vmem_limit_bytes=28 * 1024 * 1024
         ),
         name="conjugate_gradients",
     )(
@@ -505,7 +531,8 @@
         col,
         row,
         self_pairs,
-        inv_pairs,
+        inv_high,
+        inv_low,
         basis[0, 0].transpose(1, 0, 2),
         factor,
     )

time: 97.9 us -> 88.8 us (0.907)
  local copies, waits for them, and re-layouts: 18.2 us -> 8.73 us
    pallas_call x1, Pallas kernels: 16.3 us -> 20.6 us  [prepare(): pl.pallas_call(prepare_kernel, grid=(NS,), in_specs=[pl.BlockSpec((1, BZ,...]
    convert_element_type x1 -> x0, local copies, waits for them, and re-layouts: 3.5 us -> none  [per_device(): both.reshape(BZ, NS, 32, 16).transpose(1, 0, 2, 3).reshape(NS, 256, 16)]
    pallas_call x1, Pallas kernels: 60.7 us -> 57.3 us  [per_device(): pl.pallas_call(functools.partial(main_kernel, nx, ny), in_specs=[smem, sm...]
    unnamed x21 -> x13, local copies, waits for them, and re-layouts: 10.3 us -> 7.39 us
    another operation x1 -> x0, local copies, waits for them, and re-layouts: 2.68 us -> none  [per_device(): both = jnp.stack([words & 255, words >> 8], axis=-1)]
    and x1 -> x0, other arithmetic: 1.02 us -> none  [per_device(): both = jnp.stack([words & 255, words >> 8], axis=-1)]
where the time goes in v2:
time: 88.8 us; the launch traced here: 88.2 us
  Pallas kernels  77.9 us (88%)
  local copies, waits for them, and re-layouts  8.73 us (10%)
    pallas_call x1, Pallas kernels, per_device(): pl.pallas_call(functools.partial(main_kernel, nx, ny), in_specs=[smem, sm...  57.3 us
    pallas_call x1, Pallas kernels, prepare(): pl.pallas_call(prepare_kernel, grid=(NS,), in_specs=[pl.BlockSpec((1, BZ,...  20.6 us
    unnamed x13, local copies, waits for them, and re-layouts  7.39 us

profile of v2, /device:TPU:0, one launch (start us, length us, event | category | flops | bytes accessed | tf_op | source)
XLA Modules:
  0.0 88.2 jit_solution(16674194448165337900)
XLA Ops:
  0.6 0.0 copy-start.4
  0.6 0.0 copy-start.3
  0.6 0.8 reshape_squeeze.3.codes
  1.5 0.7 fusion.2
  2.2 0.1 copy.13
  2.3 0.1 select_reduce_fusion
  2.4 0.1 copy.14
  2.5 0.1 pad_slice_fusion.1
  2.6 0.1 copy.15
  2.7 0.1 reshape.72.pool_at
  2.9 1.0 %copy.18 = f32[1,1,16,8,192]{4,2,3,1,0:T(8,128)S(1)} copy(f32[1,1,16,8,192]{4,3,2,1,0:T(8,128)} %param.14) | data formatting | bytes 196608 | tf_op args[6]
  3.8 0.0 copy-start.1
  3.8 1.1 %copy-done.1 = bf16[1,1,8,36864]{3,2,1,0:T(8,128)(2,1)S(1)} copy-done((bf16[1,1,8,36864]{3,2,1,0:T(8,128)(2,1)S(1)}, bf16[1,1,8,36864]{3,2,1,0:T(8,128)(2,1)}, u32[]{:S(2)}) %copy-start.1) | copy-done | bytes 589848
  4.9 0.0 copy-start.2
  4.9 0.9 %copy-done.2 = s32[1,1,8,13,64,4]{4,5,3,2,1,0:T(4,128)S(1)} copy-done((s32[1,1,8,13,64,4]{4,5,3,2,1,0:T(4,128)S(1)}, s32[1,1,8,13,64,4]{4,5,3,2,1,0:T(4,128)}, u32[]{:S(2)}) %copy-start.2) | copy-done | bytes 106520
  5.8 20.6 %prepare.1 = (bf16[8,96,4992]{2,1,0:T(8,128)(2,1)}, f32[13,8,384]{2,1,0:T(8,128)S(1)}, f32[8,96,384]{2,1,0:T(8,128)S(1)}, bf16[8,96,384]{2,1,0:T(8,128)(2,1)S(1)...) custom-call(bf16[13,8,36864]{2,1,0:T(8,128)(2,1)} %bitcast.46, s32[8,13,4,64]{3,2,1,0:T(4,128)S(1)} %bitcast.42, ...), custom_call_target="tpu_custom_call" | custom-call | tf_op jit(solution)/shard_map/prepare/pallas_call | solution.py:99
  26.4 0.0 copy-done.4
  26.4 0.0 copy-done.3
  26.4 0.0 copy-start
  26.4 3.2 %copy-done = bf16[8,96,4992]{2,1,0:T(8,128)(2,1)S(1)} copy-done((bf16[8,96,4992]{2,1,0:T(8,128)(2,1)S(1)}, bf16[8,96,4992]{2,1,0:T(8,128)(2,1)}, u32[]{:S(2)}) %copy-start) | copy-done | bytes 7667736
  29.6 57.3 %conjugate_gradients.1 = (f32[64,192]{1,0:T(8,128)S(1)}, f32[64,192]{1,0:T(8,128)S(1)}) custom-call(s32[104]{0:T(128)S(1)} %reshape_squeeze.3.codes, s32[216]{0:T(256)S(1)} %reshape.72.pool_at, f32[64,192]{1,0:T(8,128)S(1)} %bitcast.43, bf16[8,96,4992]{2,1,0:T(8,128)(2,1)S(1)} %copy-done, f32[13,8,384]{2,1,0:T(8,128)S(1)} %get-tuple-element.11.col_in, ...), custom_call_target="tpu_custom_call" | custom-call | tf_op jit(solution)/shard_map/conjugate_gradients/pallas_call | solution.py:491
  86.9 0.6 copy.21
  87.5 0.6 copy.22
  (6 shorter events, 0.1 us)
Async XLA Ops:
  0.6 25.8 %copy-start.4 = (f32[16,512]{1,0:T(8,128)S(1)}, f32[16,512]{1,0:T(8,128)}, u32[]{:S(2)}) copy-start(f32[16,512]{1,0:T(8,128)} %factor.1) | copy-start | bytes 98308
  0.6 25.8 %copy-start.3 = (f32[1,1,8,8,192]{4,3,2,1,0:T(8,128)S(1)}, f32[1,1,8,8,192]{4,3,2,1,0:T(8,128)}, u32[]{:S(2)}) copy-start(f32[1,1,8,8,192]{4,3,2,1,0:T(8,128)} %param.8) | copy-start | bytes 147460
  3.8 1.1 %copy-start.1 = (bf16[1,1,8,36864]{3,2,1,0:T(8,128)(2,1)S(1)}, bf16[1,1,8,36864]{3,2,1,0:T(8,128)(2,1)}, u32[]{:S(2)}) copy-start(bf16[1,1,8,36864]{3,2,1,0:T(8,128)(2,1)} %param.12) | copy-start | bytes 1769476
  4.9 0.9 %copy-start.2 = (s32[1,1,8,13,64,4]{4,5,3,2,1,0:T(4,128)S(1)}, s32[1,1,8,13,64,4]{4,5,3,2,1,0:T(4,128)}, u32[]{:S(2)}) copy-start(s32[1,1,8,13,64,4]{4,5,3,2,1,0:T(4,128)} %param.10) | copy-start | bytes 319492
  26.4 3.2 %copy-start = (bf16[8,96,4992]{2,1,0:T(8,128)(2,1)S(1)}, bf16[8,96,4992]{2,1,0:T(8,128)(2,1)}, u32[]{:S(2)}) copy-start(bf16[8,96,4992]{2,1,0:T(8,128)(2,1)} %get-tuple-element.10.w_hbm) | copy-start | bytes 23003140

commit v3 on v2

--- a/solution.py
+++ b/solution.py
@@ -41,7 +41,7 @@
 
 
 def prepare_kernel(
-    bond, words, self_flat, inv_flat, w_out, col_out, row_out, self_out, inv_hi, inv_lo, scr, place
+    bond, words, self_flat, inv_flat, w_out, col_out, self_out, inv_hi, inv_lo, scr, place
 ):
     step = pl.program_id(0)
 
@@ -54,7 +54,6 @@
 
     @pl.when(step == 0)
     def _():
-        row_out[...] = jnp.zeros_like(row_out)
         point, at = iota((512, 512), 0), iota((512, 512), 1)
         to = at % 256
         place[...] = (point == (to // 32) * 64 + (to % 32) * 2 + at // 256).astype(BF16)
@@ -72,7 +71,8 @@
                     pl.ds(t * 8 + z, HALF, stride=24), :
                 ].astype(BF16)
 
-    spread(lambda lanes: bond[0, :, lanes].astype(F32))
+    for k in range(288):
+        scr[k * 8 : k * 8 + 8, :] = bond[0, :, k * 128 : k * 128 + 128].astype(F32)
     lane = iota((16, PAIR), 1)
     column = lane % DOF % 64
     code = (lane // DOF) * 8 + (column % 16) // 8 * 4 + column // 16
@@ -90,7 +90,6 @@
             mask = keep[z * 32 : (z + 1) * 32, lanes]
             part = scr[pl.ds(t * 8 + z, HALF, stride=24), :] * jnp.concatenate([mask] * 3, axis=0)
             w_out[z, :, lanes] = part.astype(BF16)
-            row_out[z, :, lanes] += part
             col_out[0, z : z + 1, lanes] = jnp.sum(part, axis=0, keepdims=True)
 
 
@@ -111,18 +110,16 @@
             whole(BZ, HALF, PAIR),
             whole(BZ, HALF, PAIR),
             whole(BZ, HALF, PAIR),
-            whole(BZ, HALF, PAIR),
         ],
         out_shape=[
             jax.ShapeDtypeStruct((BZ, HALF, NS * PAIR), BF16),
             jax.ShapeDtypeStruct((NS, BZ, PAIR), F32),
-            jax.ShapeDtypeStruct((BZ, HALF, PAIR), F32),
             jax.ShapeDtypeStruct((BZ, HALF, PAIR), BF16),
             jax.ShapeDtypeStruct((BZ, HALF, PAIR), BF16),
             jax.ShapeDtypeStruct((BZ, HALF, PAIR), BF16),
         ],
         scratch_shapes=[pltpu.VMEM((288 * 8, 128), F32), pltpu.VMEM((512, 512), BF16)],
-        compiler_params=pltpu.CompilerParams(vmem_limit_bytes=50 * 1024 * 1024),
+        compiler_params=pltpu.CompilerParams(vmem_limit_bytes=59 * 1024 * 1024),
         name="prepare",
     )(bond, words, self_flat, inv_flat)
 
@@ -135,7 +132,6 @@
     load,
     w_hbm,
     col_in,
-    row_in,
     self_in,
     inv_high,
     inv_low,
@@ -248,6 +244,8 @@
     def pick(packed, k):
         return jnp.sum(jnp.where(lane == k, packed, 0.0), axis=1, keepdims=True)
 
+    sent = []
+
     def all_sum(turn, width, beside=lambda: None):
         for buf, send_sem, recv_sem, me, size, axis in (
             (sum_y, y_send_sem, y_recv_sem, me_y, ny, 1),
@@ -271,8 +269,7 @@
                 beside()
             for copy in copies:
                 copy.wait_recv()
-            for copy in copies:
-                copy.wait_send()
+            sent.extend(copies)
             total = buf[turn, 0, :, :width]
             for j in range(1, size):
                 total = total + buf[turn, j, :, :width]
@@ -335,8 +332,10 @@
             wide[n * SPAN + SPAN - 1] = jnp.zeros((16, PAIR), F32)
         for z in range(BZ):
             terms[z * SLOTS + NS] = jnp.zeros((NLOAD, DOF), F32)
-        ones = ((iota((16, PAIR), 1) < DOF) == (iota((16, PAIR), 0) < NLOAD)).astype(F32)
-        sums = jnp.concatenate([dot_t(row_in[z], ones, HI) for z in range(BZ)], axis=1)
+        every = (16, NS * PAIR)
+        ones = ((iota(every, 1) % PAIR < DOF) == (iota(every, 0) < NLOAD)).astype(F32).astype(BF16)
+        load_w.wait()
+        sums = jnp.concatenate([dot_t(w[z], ones) for z in range(BZ)], axis=1)
         row_sum[...] = sums.T
         for s in range(NS):
             both = col_in[s]
@@ -364,8 +363,6 @@
         odd = dot(rounded, to_odd)
         even_img[...] = even
         odd_img[...] = odd
-        if turn == 0:
-            load_w.wait()
 
         @pl.loop(0, BZ)
         def _(z):
@@ -468,6 +465,8 @@
     step_all = tiled(new_energy / pick(all_sum(2, 128), 0))
     disp_out[...] = moved + step_all * direction
     res_out[...] = residual - step_all * out
+    for copy in sent:
+        copy.wait_send()
 
 
 def per_device(load, bond, words, block_cols, self_flat, inv_flat, basis, factor):
@@ -482,7 +481,7 @@
     pool_at = jnp.stack([table[2 - b : 2 - b + BZ, :, b] for b in range(3)], axis=-1)
     pool_at = pool_at.transpose(1, 0, 2).reshape(-1)
 
-    w, col, row, self_pairs, inv_high, inv_low = prepare(
+    w, col, self_pairs, inv_high, inv_low = prepare(
         bond[0, 0].transpose(1, 0, 2), words[0, 0].transpose(0, 1, 3, 2), self_flat[0, 0], inv_flat[0, 0]
     )
     vmem = pl.BlockSpec(memory_space=pltpu.VMEM)
@@ -490,7 +489,7 @@
     dma = pltpu.SemaphoreType.DMA
     disp, res = pl.pallas_call(
         functools.partial(main_kernel, nx, ny),
-        in_specs=[smem, smem, vmem, pl.BlockSpec(memory_space=pl.ANY)] + [vmem] * 7,
+        in_specs=[smem, smem, vmem, pl.BlockSpec(memory_space=pl.ANY)] + [vmem] * 6,
         out_specs=[vmem, vmem],
         out_shape=[jax.ShapeDtypeStruct((ROWS, DOF), F32)] * 2,
         scratch_shapes=[
@@ -520,7 +519,7 @@
             dma((3, nx)),
         ],
         compiler_params=pltpu.CompilerParams(
-            collective_id=0, has_side_effects=True, vmem_limit_bytes=28 * 1024 * 1024
+            collective_id=0, has_side_effects=True, vmem_limit_bytes=59 * 1024 * 1024
         ),
         name="conjugate_gradients",
     )(
@@ -529,7 +528,6 @@
         load.reshape(ROWS, DOF),
         w,
         col,
-        row,
         self_pairs,
         inv_high,
         inv_low,

time: 88.8 us -> 84.8 us (0.955)
  Pallas kernels: 77.9 us -> 75.7 us
  local copies, waits for them, and re-layouts: 8.73 us -> 6.93 us
    pallas_call x1, Pallas kernels: 20.6 us -> 17.5 us  [prepare(): pl.pallas_call(prepare_kernel, grid=(NS,), in_specs=[pl.BlockSpec((1, BZ,...]
    unnamed x13 -> x3, local copies, waits for them, and re-layouts: 7.39 us -> 4.54 us
    pallas_call x1, Pallas kernels: 57.3 us -> 58.2 us  [per_device(): pl.pallas_call(functools.partial(main_kernel, nx, ny), in_specs=[smem, sm...]
where the time goes in v3:
time: 84.8 us; the launch traced here: 84.1 us
  Pallas kernels  75.7 us (89%)
  local copies, waits for them, and re-layouts  6.93 us (8%)
    pallas_call x1, Pallas kernels, per_device(): pl.pallas_call(functools.partial(main_kernel, nx, ny), in_specs=[smem, sm...  58.2 us
    pallas_call x1, Pallas kernels, prepare(): pl.pallas_call(prepare_kernel, grid=(NS,), in_specs=[pl.BlockSpec((1, BZ,...  17.5 us
    unnamed x3, local copies, waits for them, and re-layouts  4.54 us

profile of v3, /device:TPU:0, one launch (start us, length us, event | category | flops | bytes accessed | tf_op | source)
XLA Modules:
  0.0 84.1 jit_solution(6509658859965759888)
XLA Ops:
  0.6 1.3 %reshape_squeeze.3.codes = s32[104]{0:T(128)} reshape(s32[1,1,8,13]{3,2,1,0:T(8,128)} %param.11) | data formatting | bytes 832 | tf_op jit(solution)/shard_map/reshape;squeeze | solution.py:526
  1.9 0.7 fusion.2
  2.6 0.1 copy.13
  2.7 0.1 select_reduce_fusion
  2.8 0.1 copy.14
  2.9 0.1 pad_slice_fusion.1
  3.0 0.1 copy.15
  3.2 0.7 reshape.72.pool_at
  3.9 1.6 %copy.18 = f32[1,1,16,8,192]{4,2,3,1,0:T(8,128)} copy(f32[1,1,16,8,192]{4,3,2,1,0:T(8,128)} %param.14) | data formatting | bytes 196608 | tf_op args[6]
  5.5 17.5 %prepare.1 = (bf16[8,96,4992]{2,1,0:T(8,128)(2,1)}, f32[13,8,384]{2,1,0:T(8,128)}, bf16[8,96,384]{2,1,0:T(8,128)(2,1)}, bf16[8,96,384]{2,1,0:T(8,128)(2,1)}, bf16[8,96,384]{2,1,0:T(8,128)(2,1)}) custom-call(bf16[13,8,36864]{2,1,0:T(8,128)(2,1)} %bitcast.40, s32[8,13,4,64]{3,2,1,0:T(4,128)} %bitcast.44, bf16[8,36864]{1,0:T(8,128)(2,1)} %bitcast.42, ...), custom_call_target="tpu_custom_call" | custom-call | tf_op jit(solution)/shard_map/prepare/pallas_call | solution.py:98
  23.0 58.2 %conjugate_gradients.1 = (f32[64,192]{1,0:T(8,128)}, f32[64,192]{1,0:T(8,128)}) custom-call(s32[104]{0:T(128)} %reshape_squeeze.3.codes, s32[216]{0:T(256)} %reshape.72.pool_at, f32[64,192]{1,0:T(8,128)} %bitcast.45, bf16[8,96,4992]{2,1,0:T(8,128)(2,1)} %get-tuple-element.9.w_hbm, f32[13,8,384]{2,1,0:T(8,128)} %get-tuple-element.10.col_in, ...), custom_call_target="tpu_custom_call" | custom-call | tf_op jit(solution)/shard_map/conjugate_gradients/pallas_call | solution.py:490
  81.2 1.5 %copy.21 = f32[1,1,8,8,192]{4,3,2,1,0:T(8,128)} copy(f32[1,1,8,8,192]{4,3,2,1,0:T(8,128)} %bitcast.47) | data formatting | bytes 98304
  82.7 1.5 %copy.22 = f32[1,1,8,8,192]{4,3,2,1,0:T(8,128)} copy(f32[1,1,8,8,192]{4,3,2,1,0:T(8,128)} %bitcast.46) | data formatting | bytes 98304
  (6 shorter events, 0.1 us)
